TPU v7x, 32 devices: a whole 2x2x4 slice. The times are simulated.
32 devices in a mesh: dp: 8 (over y, x, core), tensor: 4 (over z).
Axes of the slice: x: 2, y: 2, z: 4, core: 2. Of those that a mesh axis runs over, the one named last changes fastest.
Arguments:
- tokens: bfloat16 [8192, 1024], P(('dp', 'tensor')), may hold values from -6 to 6
- cotangent: bfloat16 [8192, 1024], P(('dp', 'tensor')), may hold values from -6 to 6
- segments: int32 [8, 1024], P('dp'), may hold values from 0 to 3, never falling along the last dimension, each value on 1 to 800 neighbouring positions
- norm_gains: bfloat16 [2, 1024], replicated, may hold values from 0.5 to 1.5
- mixer_in: bfloat16 [1024, 6144], P('dp', 'tensor'), may hold values from -0.1875 to 0.1875
- mixer_small: bfloat16 [2, 1024, 8], P(None, 'dp', 'tensor'), may hold values from -0.1875 to 0.1875
- conv_weight: bfloat16 [4, 8, 512], P(None, 'tensor', 'dp'), may hold values from -3 to 3
- head_params: float32 [2, 8], replicated, may hold values from -10 to 3, as said below
- out_norm: bfloat16 [8, 256], P('tensor', 'dp'), may hold values from 0.5 to 1.5
- mixer_out: bfloat16 [2048, 1024], P('tensor', 'dp'), may hold values from -0.125 to 0.125
- ffn_in: bfloat16 [2, 1024, 2816], P(None, 'dp', 'tensor'), may hold values from -0.1875 to 0.1875
- ffn_out: bfloat16 [2816, 1024], P('tensor', 'dp'), may hold values from -0.109375 to 0.109375
Outputs:
- output: bfloat16 [8192, 1024], P(('dp', 'tensor'))
- grad_tokens: float32 [8192, 1024], P(('dp', 'tensor'))
- grad_norm_gains: float32 [2, 1024], replicated
- grad_mixer_in: float32 [1024, 6144], P('dp', 'tensor')
- grad_mixer_small: float32 [2, 1024, 8], P(None, 'dp', 'tensor')
- grad_conv_weight: float32 [4, 8, 512], P(None, 'tensor', 'dp')
- grad_head_params: float32 [2, 8], replicated
- grad_out_norm: float32 [8, 256], P('tensor', 'dp')
- grad_mixer_out: float32 [2048, 1024], P('tensor', 'dp')
- grad_ffn_in: float32 [2, 1024, 2816], P(None, 'dp', 'tensor')
- grad_ffn_out: float32 [2816, 1024], P('tensor', 'dp')
Inputs may be any that keep to these rules, and one draw needn't show every extreme that they name: `segments`: within each sequence the numbers never fall; each document has 1 to 800 tokens and some document has exactly 800. `head_params`: row 0 is the logarithm of each head's decay rate, row 1 the bias added before the softplus.
All inputs are finite; a program needn't handle non-finite values.
Results may differ from a plain program's by a relative error of at most 0.019.
Values may be sent and summed in bfloat16 or wider, within the bound.
No kernel may reach another device: no remote copies, remote signals or barrier semaphores. Data moves between devices by JAX's collectives and lax.ppermute only.
A program may use at most 192 MiB of HBM per device.

v0:
```python
import jax
import jax.numpy as jnp
from jax import lax
from jax.sharding import PartitionSpec as P

DK = 128
DV = 256
SPAN = 64


highest = lax.Precision.HIGHEST


def block_step(state, blocks):
    query, key_end, carried, carried_last, attend, fixed, across = blocks
    deltas = fixed - jnp.einsum("bhid,bhde->bhie", across, state, precision=highest)
    result = carried[..., None] * jnp.einsum("bhid,bhde->bhie", query, state, precision=highest)
    result = result + jnp.einsum("bhij,bhje->bhie", attend, deltas, precision=highest)
    new_state = carried_last[..., None, None] * state
    new_state = new_state + jnp.einsum("bhjd,bhje->bhde", key_end, deltas, precision=highest)
    return (new_state, result)


def to_blocks(values, nseq, count):
    return values.reshape(nseq, count, SPAN, values.shape[2], values.shape[3]).transpose(
        1, 0, 3, 2, 4
    )


def delta_rule(query, key, value, beta, log_decay, seg):
    nseq, length, heads = beta.shape
    count = length // SPAN
    query_b = to_blocks(query, nseq, count)
    key_b = to_blocks(key, nseq, count)
    value_b = to_blocks(value, nseq, count)
    beta_b = beta.reshape(nseq, count, SPAN, heads).transpose(1, 0, 3, 2)
    decay_b = log_decay.reshape(nseq, count, SPAN, heads).transpose(1, 0, 3, 2)
    seg_b = seg.reshape(nseq, count, SPAN).transpose(1, 0, 2)
    before = jnp.concatenate([jnp.full((1, nseq), -1, jnp.int32), seg_b[:-1, :, SPAN - 1]], 0)
    total = jnp.cumsum(decay_b, -1)
    row_ids = lax.broadcasted_iota(jnp.int32, (SPAN, SPAN), 0)
    col_ids = lax.broadcasted_iota(jnp.int32, (SPAN, SPAN), 1)
    same = (seg_b[..., :, None] == seg_b[..., None, :])[:, :, None]
    keep_mask = same & (row_ids >= col_ids)
    differ = total[..., :, None] - total[..., None, :]
    decay = jnp.where(keep_mask, jnp.exp(jnp.where(keep_mask, differ, 0.0)), 0.0)
    carried = jnp.where((seg_b == before[..., None])[:, :, None], jnp.exp(total), 0.0)
    inner_kk = jnp.einsum("abhid,abhjd->abhij", key_b, key_b, precision=highest)
    strict = jnp.where(row_ids > col_ids, decay, 0.0)
    lower_mat = beta_b[..., None] * strict * inner_kk + jnp.where(row_ids == col_ids, 1.0, 0.0)
    sides = jnp.concatenate(
        [beta_b[..., None] * value_b, (beta_b * carried)[..., None] * key_b], -1
    )
    solved = lax.linalg.triangular_solve(
        lower_mat, sides, left_side=True, lower=True, unit_diagonal=True
    )
    fixed = solved[..., :DV]
    across = solved[..., DV:]
    inner_qk = jnp.einsum("abhid,abhjd->abhij", query_b, key_b, precision=highest)
    attend = decay * inner_qk
    key_end = key_b * decay[..., SPAN - 1, :][..., None]
    carried_last = carried[..., SPAN - 1]
    state = jnp.zeros((nseq, heads, DK, DV), jnp.float32)
    unused, outputs = lax.scan(
        jax.checkpoint(block_step),
        state,
        (query_b, key_end, carried, carried_last, attend, fixed, across),
    )
    return outputs.transpose(1, 0, 3, 2, 4).reshape(nseq, length, heads, DV)


def mixer_core(proj, small, conv, head, onorm, seg):
    nseq, length = seg.shape
    heads = proj.shape[1]
    width = conv.shape[0]
    mixed_in = proj[:, :, : 2 * DK + DV].reshape(nseq, length, heads, 2 * DK + DV)
    gate = proj[:, :, 2 * DK + DV :].reshape(nseq, length, heads, DV)
    seg_pad = jnp.pad(seg, ((0, 0), (width - 1, 0)), constant_values=-1)
    in_pad = jnp.pad(mixed_in, ((0, 0), (width - 1, 0), (0, 0), (0, 0)))
    mixed = jnp.zeros_like(mixed_in)
    for shift in range(width):
        begin = width - 1 - shift
        same = (seg_pad[:, begin : begin + length] == seg)[:, :, None, None]
        mixed = mixed + conv[width - 1 - shift] * jnp.where(
            same, in_pad[:, begin : begin + length], 0.0
        )
    active = jax.nn.silu(mixed)
    query = active[..., :DK]
    key = active[..., DK : 2 * DK]
    value = active[..., 2 * DK :]
    query = query * lax.rsqrt(jnp.sum(query * query, -1, keepdims=True) + 1e-06) * DK ** (-0.5)
    key = key * lax.rsqrt(jnp.sum(key * key, -1, keepdims=True) + 1e-06)
    beta = jax.nn.sigmoid(small[:, 0, :]).reshape(nseq, length, heads)
    log_decay = (-jnp.exp(head[0]) * jax.nn.softplus(small[:, 1, :] + head[1])).reshape(
        nseq, length, heads
    )
    result = delta_rule(query, key, value, beta, log_decay, seg)
    factor = lax.rsqrt(jnp.mean(result * result, -1, keepdims=True) + 1e-05)
    return (result * factor * onorm * jax.nn.silu(gate)).reshape(nseq * length, heads * DV)


def norm_factor(values):
    return lax.rsqrt(jnp.mean(values * values, -1, keepdims=True) + 1e-06)


def norm_backward(grad_out, scaled, factor, gain):
    grad_scaled = grad_out * gain
    grad_input = factor * (grad_scaled - scaled * jnp.mean(grad_scaled * scaled, -1, keepdims=True))
    return (grad_input, jnp.sum(grad_out * scaled, 0))


def fetch_mixer(mixer_in, mixer_small, conv_weight, out_norm, mixer_out):
    return (
        lax.all_gather(mixer_in, "dp", axis=0, tiled=True),
        lax.all_gather(mixer_small, "dp", axis=1, tiled=True),
        lax.all_gather(conv_weight, "dp", axis=2, tiled=True),
        lax.all_gather(out_norm, "dp", axis=1, tiled=True),
        lax.all_gather(mixer_out, "dp", axis=1, tiled=True),
    )


def fetch_ffn(ffn_in, ffn_out):
    return (
        lax.all_gather(ffn_in, "dp", axis=1, tiled=True),
        lax.all_gather(ffn_out, "dp", axis=1, tiled=True),
    )


def shards(
    tokens,
    cotangent,
    segments,
    norm_gains,
    mixer_in,
    mixer_small,
    conv_weight,
    head_params,
    out_norm,
    mixer_out,
    ffn_in,
    ffn_out,
):
    local_heads = mixer_in.shape[1] // (2 * DK + 2 * DV)
    all_heads = head_params.shape[1]
    head_start = lax.axis_index("tensor") * local_heads
    head_local = lax.dynamic_slice_in_dim(head_params, head_start, local_heads, 1)
    gains = norm_gains.astype(jnp.float32)
    inputs = tokens.astype(jnp.float32)
    factor_one = norm_factor(inputs)
    scaled_one = inputs * factor_one
    normed_one = (scaled_one * gains[0]).astype(jnp.bfloat16)
    rows_one = lax.all_gather(normed_one, "tensor", axis=0, tiled=True)
    group = rows_one.shape[0]
    w_in, w_small, w_conv, w_onorm, w_out = fetch_mixer(
        mixer_in, mixer_small, conv_weight, out_norm, mixer_out
    )
    proj = jnp.dot(rows_one, w_in, preferred_element_type=jnp.float32).reshape(
        group, local_heads, 2 * DK + 2 * DV
    )
    small = jnp.einsum("nd,cdh->nch", rows_one, w_small, preferred_element_type=jnp.float32)

    def core(proj_value, small_value, conv_value, head_value, onorm_value):
        return mixer_core(proj_value, small_value, conv_value, head_value, onorm_value, segments)

    mixed = core(
        proj, small, w_conv.astype(jnp.float32), head_local, w_onorm.astype(jnp.float32)
    ).astype(jnp.bfloat16)
    middle = inputs + lax.psum_scatter(
        jnp.dot(mixed, w_out, preferred_element_type=jnp.float32).astype(jnp.bfloat16),
        "tensor",
        scatter_dimension=0,
        tiled=True,
    ).astype(jnp.float32)
    factor_two = norm_factor(middle)
    scaled_two = middle * factor_two
    normed_two = (scaled_two * gains[1]).astype(jnp.bfloat16)
    rows_two = lax.all_gather(normed_two, "tensor", axis=0, tiled=True)
    w_ffn, w_down = fetch_ffn(ffn_in, ffn_out)
    both = jnp.einsum("nd,cdf->ncf", rows_two, w_ffn, preferred_element_type=jnp.float32)
    gate_part = both[:, 0]
    up_part = both[:, 1]
    sigma = jax.nn.sigmoid(gate_part)
    activ = gate_part * sigma
    hidden = (activ * up_part).astype(jnp.bfloat16)
    result = middle + lax.psum_scatter(
        jnp.dot(hidden, w_down, preferred_element_type=jnp.float32).astype(jnp.bfloat16),
        "tensor",
        scatter_dimension=0,
        tiled=True,
    ).astype(jnp.float32)
    grad_rows = lax.all_gather(cotangent, "tensor", axis=0, tiled=True)
    w_ffn, w_down = fetch_ffn(ffn_in, ffn_out)
    grad_hidden = jnp.einsum("nd,fd->nf", grad_rows, w_down, preferred_element_type=jnp.float32)
    grad_down = jnp.einsum("nf,nd->fd", hidden, grad_rows, preferred_element_type=jnp.float32)
    grad_gate = grad_hidden * up_part * sigma * (1.0 + gate_part * (1.0 - sigma))
    grad_up = grad_hidden * activ
    grad_both = jnp.stack([grad_gate, grad_up], 1).astype(jnp.bfloat16)
    grad_ffn = jnp.einsum("nd,ncf->cdf", rows_two, grad_both, preferred_element_type=jnp.float32)
    grad_normed_two = lax.psum_scatter(
        jnp.einsum("ncf,cdf->nd", grad_both, w_ffn, preferred_element_type=jnp.float32).astype(
            jnp.bfloat16
        ),
        "tensor",
        scatter_dimension=0,
        tiled=True,
    ).astype(jnp.float32)
    grad_middle_norm, grad_gain_two = norm_backward(
        grad_normed_two, scaled_two, factor_two, gains[1]
    )
    grad_middle = cotangent.astype(jnp.float32) + grad_middle_norm
    ffn_grads = (
        lax.psum_scatter(
            grad_ffn.astype(jnp.bfloat16), "dp", scatter_dimension=1, tiled=True
        ).astype(jnp.float32),
        lax.psum_scatter(
            grad_down.astype(jnp.bfloat16), "dp", scatter_dimension=1, tiled=True
        ).astype(jnp.float32),
    )
    branch_grad = lax.all_gather(grad_middle.astype(jnp.bfloat16), "tensor", axis=0, tiled=True)
    w_in, w_small, w_conv, w_onorm, w_out = fetch_mixer(
        mixer_in, mixer_small, conv_weight, out_norm, mixer_out
    )
    grad_mixed = jnp.einsum("nd,kd->nk", branch_grad, w_out, preferred_element_type=jnp.float32)
    grad_out = jnp.einsum("nk,nd->kd", mixed, branch_grad, preferred_element_type=jnp.float32)
    unused, pullback = jax.vjp(
        core, proj, small, w_conv.astype(jnp.float32), head_local, w_onorm.astype(jnp.float32)
    )
    grad_proj, grad_small, grad_conv, grad_head, grad_onorm = pullback(grad_mixed)
    grad_proj = grad_proj.reshape(group, local_heads * (2 * DK + 2 * DV)).astype(jnp.bfloat16)
    grad_small = grad_small.astype(jnp.bfloat16)
    grad_in = jnp.einsum("nd,nk->dk", rows_one, grad_proj, preferred_element_type=jnp.float32)
    grad_small_w = jnp.einsum(
        "nd,nch->cdh", rows_one, grad_small, preferred_element_type=jnp.float32
    )
    total = jnp.einsum("nk,dk->nd", grad_proj, w_in, preferred_element_type=jnp.float32)
    grad_normed_one = lax.psum_scatter(
        (
            total
            + jnp.einsum("nch,cdh->nd", grad_small, w_small, preferred_element_type=jnp.float32)
        ).astype(jnp.bfloat16),
        "tensor",
        scatter_dimension=0,
        tiled=True,
    ).astype(jnp.float32)
    grad_input_norm, grad_gain_one = norm_backward(
        grad_normed_one, scaled_one, factor_one, gains[0]
    )
    grad_tokens = grad_middle + grad_input_norm
    mixer_grads = (
        lax.psum_scatter(
            grad_in.astype(jnp.bfloat16), "dp", scatter_dimension=0, tiled=True
        ).astype(jnp.float32),
        lax.psum_scatter(
            grad_small_w.astype(jnp.bfloat16), "dp", scatter_dimension=1, tiled=True
        ).astype(jnp.float32),
        lax.psum_scatter(
            grad_conv.astype(jnp.bfloat16), "dp", scatter_dimension=2, tiled=True
        ).astype(jnp.float32),
        lax.psum_scatter(
            grad_onorm.astype(jnp.bfloat16), "dp", scatter_dimension=1, tiled=True
        ).astype(jnp.float32),
        lax.psum_scatter(
            grad_out.astype(jnp.bfloat16), "dp", scatter_dimension=1, tiled=True
        ).astype(jnp.float32),
    )
    head_full = lax.dynamic_update_slice_in_dim(
        jnp.zeros((2, all_heads), jnp.float32), grad_head, head_start, 1
    )
    gain_total, head_total = lax.psum(
        (jnp.stack([grad_gain_one, grad_gain_two]), head_full), ("dp", "tensor")
    )
    return (
        result.astype(jnp.bfloat16),
        grad_tokens,
        gain_total,
        mixer_grads[0],
        mixer_grads[1],
        mixer_grads[2],
        head_total,
        mixer_grads[3],
        mixer_grads[4],
        ffn_grads[0],
        ffn_grads[1],
    )


def solution(mesh):
    in_specs = (
        P(("dp", "tensor"), None),
        P(("dp", "tensor"), None),
        P("dp", None),
        P(),
        P("dp", "tensor"),
        P(None, "dp", "tensor"),
        P(None, "tensor", "dp"),
        P(),
        P("tensor", "dp"),
        P("tensor", "dp"),
        P(None, "dp", "tensor"),
        P("tensor", "dp"),
    )
    out_specs = (
        P(("dp", "tensor"), None),
        P(("dp", "tensor"), None),
        P(),
        P("dp", "tensor"),
        P(None, "dp", "tensor"),
        P(None, "tensor", "dp"),
        P(),
        P("tensor", "dp"),
        P("tensor", "dp"),
        P(None, "dp", "tensor"),
        P("tensor", "dp"),
    )
    return jax.shard_map(shards, mesh=mesh, in_specs=in_specs, out_specs=out_specs, check_vma=False)
```

profile of v0, /device:TPU:0, one launch (start us, length us, event | category | flops | bytes accessed | tf_op | source)
XLA Modules:
  0.0 1638.6 jit_solution(17017068100295244218)
XLA Ops:
  15.5 10.8 all_gather.42
  28.3 8.8 all_gather.41
  48.3 12.4 all-gather.10.cloned.1.call-done
  67.5 26.1 %all-gather.12.cloned.1.call-done = bf16[1024,1536]{1,0:T(8,128)(2,1)} async-done(((bf16[128,1536]{1,0:T(8,128)(2,1)}), bf16[1024,1536]{1,0:T(8,128)(2,1)}) %all-gather.12.cloned.1.call-update) | async-done | bytes 3145744 | tf_op jit(solution)/shard_map/all_gather | solution.py:114
  93.6 8.6 fusion.244
  129.4 158.8 %custom-call.12 = f32[16,1,2,1,64,64]{4,5,3,2,1,0:T(8,128)} custom-call(f32[16,1,2,1,64,64]{5,4,3,2,1,0:T(8,128)} %get-tuple-element.1005), custom_call_target="InvertDiagBlocksLowerTriangular" | custom-call | tf_op jit(solution)/shard_map/triangular_solve/custom-call.1 | solution.py:54
  304.6 107.1 %while.57 = (s32[]{:T(128)}, f32[1,2,128,256]{3,2,1,0:T(8,128)S(1)}, f32[16,1,2,64,256]{4,3,0,2,1:T(8,128)}, f32[16,1,2]{2,1,0:T(1,128)}, f32[16,1,2,64,128]{4,3...) while((s32[]{:T(128)}, ...), condition=%wide.region_5.7_spmd.clone, body=%wide.region_4.6_spmd.clone.sunk | while | flops 176586752 | bytes 2232993 | solution.py:64
  426.5 43.3 %reduce-scatter.24.cloned.1.call-done = bf16[256,1024]{1,0:T(8,128)(2,1)} async-done(((bf16[1024,1024]{1,0:T(8,128)(2,1)}), bf16[256,1024]{1,0:T(8,128)(2,1)}) %reduce-scatter.24.cloned.1.call-update) | async-done | bytes 524304 | tf_op jit(solution)/shard_map/reduce_scatter | solution.py:168
  475.4 27.3 %all-gather.18.cloned.1.call-done = bf16[2,1024,704]{1,2,0:T(8,128)(2,1)} async-done(((bf16[2,128,704]{1,2,0:T(8,128)(2,1)}), bf16[2,1024,704]{1,2,0:T(8,128)(2,1)}) %all-gather.18.cloned.1.call-update) | async-done | bytes 2883600 | tf_op jit(solution)/shard_map/all_gather | solution.py:124
  502.7 48.0 %all-gather.16.cloned.1.call-done = bf16[1024,1024]{1,0:T(8,128)(2,1)} async-done(((bf16[256,1024]{1,0:T(8,128)(2,1)}), bf16[1024,1024]{1,0:T(8,128)(2,1)}) %all-gather.16.cloned.1.call-update) | async-done | bytes 2097168 | tf_op jit(solution)/shard_map/all_gather | solution.py:177
  558.8 18.0 %all-gather.20.cloned.1.call-done = bf16[704,1024]{1,0:T(8,128)(2,1)} async-done(((bf16[704,128]{1,0:T(8,128)(2,1)}), bf16[704,1024]{1,0:T(8,128)(2,1)}) %all-gather.20.cloned.1.call-update) | async-done | bytes 1441808 | tf_op jit(solution)/shard_map/all_gather | solution.py:125
  576.8 47.6 %all-gather.22.cloned.1.call-done = bf16[1024,1024]{1,0:T(8,128)(2,1)} async-done(((bf16[256,1024]{1,0:T(8,128)(2,1)}), bf16[1024,1024]{1,0:T(8,128)(2,1)}) %all-gather.22.cloned.1.call-update) | async-done | bytes 2097168 | tf_op jit(solution)/shard_map/all_gather | solution.py:191
  638.5 42.7 %reduce-scatter.28.cloned.1.call-done = bf16[256,1024]{1,0:T(8,128)(2,1)} async-done(((bf16[1024,1024]{1,0:T(8,128)(2,1)}), bf16[256,1024]{1,0:T(8,128)(2,1)}) %reduce-scatter.28.cloned.1.call-update) | async-done | bytes 524304 | tf_op jit(solution)/shard_map/reduce_scatter | solution.py:199
  697.0 118.8 %while.58 = (s32[]{:T(128)}, f32[1,2,128,256]{3,2,1,0:T(8,128)S(1)}, f32[16,1,2,64,256]{4,3,0,2,1:T(8,128)}, f32[16,1,2,128,256]{4,3,2,1,0:T(8,128)}, f32[16,1,2...) while((s32[]{:T(128)}, ...), condition=%wide.region_13.15_spmd.clone, body=%wide.region_12.14_spmd.clone.sunk | while | flops 176652288 | bytes 2757802 | solution.py:64
  817.9 158.7 %custom-call.8 = f32[16,1,2,1,64,64]{4,5,3,2,1,0:T(8,128)} custom-call(f32[16,1,2,1,64,64]{5,4,3,2,1,0:T(8,128)} %get-tuple-element.1004), custom_call_target="InvertDiagBlocksLowerTriangular" | custom-call | tf_op jit(solution)/shard_map/transpose(jvp())/triangular_solve | solution.py:54
  983.7 8.7 copy.499
  1020.7 267.7 %while.59 = (s32[]{:T(128)}, f32[1,2,128,256]{2,3,1,0:T(8,128)S(1)}, f32[16,1,2,64,128]{4,3,2,1,0:T(8,128)}, f32[16,1,2,64,128]{4,3,2,1,0:T(8,128)}, f32[16,1,2,...) while((s32[]{:T(128)}, ...), condition=%wide.region_19.21_spmd.clone, body=%wide.region_16.20_spmd.clone.sunk | while | flops 453640064 | bytes 8491407 | solution.py:64
  1326.6 8.6 multiply_reduce_fusion.4
  1389.0 22.5 %reduce-scatter.36.cloned.1.call-done = bf16[64,8]{1,0:T(8,128)(2,1)} async-done(((bf16[512,8]{1,0:T(8,128)(2,1)}), bf16[64,8]{1,0:T(8,128)(2,1)}) %reduce-scatter.36.cloned.1.call-update) | async-done | bytes 1040
  1413.0 35.8 %reduce-scatter.34.cloned.1.call-done = bf16[128,4]{1,0:T(8,128)(2,1)} async-done(((bf16[1024,4]{1,0:T(8,128)(2,1)}), bf16[128,4]{1,0:T(8,128)(2,1)}) %reduce-scatter.34.cloned.1.call-update) | async-done | bytes 1040
  1450.4 38.1 %reduce-scatter.40.cloned.1.call-done = bf16[128,512]{1,0:T(8,128)(2,1)} async-done(((bf16[1024,512]{1,0:T(8,128)(2,1)}), bf16[128,512]{1,0:T(8,128)(2,1)}) %reduce-scatter.40.cloned.1.call-update) | async-done | bytes 131088
  1490.2 44.3 %reduce-scatter.30.cloned.1.call-done = bf16[256,1024]{1,0:T(8,128)(2,1)} async-done(((bf16[1024,1024]{1,0:T(8,128)(2,1)}), bf16[256,1024]{1,0:T(8,128)(2,1)}) %reduce-scatter.30.cloned.1.call-update) | async-done | bytes 524304 | tf_op jit(solution)/shard_map/reduce_scatter | solution.py:236
  1536.1 42.5 %all-reduce.23 = (f32[2,1024]{1,0:T(2,128)}, f32[2,8]{1,0:T(2,128)}) all-reduce(f32[2,1024]{1,0:T(2,128)S(1)} %pad_maximum_fusion.3, f32[2,8]{1,0:T(2,128)S(1)} %dynamic_update_slice.81), channel_id=1, replica_groups=mesh['dp'=8,'tensor'=4] {'dp','tensor'}, use_global_device_ids=true, to_apply=%region_33.35 | all-reduce | flops 2064 | bytes 16512 | tf_op jit(solution)/shard_map/psum | solution.py:269
  1584.2 45.6 %reduce-scatter.32.cloned.1.call-done = bf16[128,1536]{1,0:T(8,128)(2,1)} async-done(((bf16[1024,1536]{1,0:T(8,128)(2,1)}), bf16[128,1536]{1,0:T(8,128)(2,1)}) %reduce-scatter.32.cloned.1.call-update) | async-done | bytes 393232 | tf_op jit(solution)/shard_map/reduce_scatter | solution.py:250
  (1095 shorter events, 762.6 us)
Async XLA Ops:
  7.2 53.5 %all-gather.10.cloned.1.call-start = ((), (), s32[]{:S(2)}) async-start(), calls=%async_computation.11 | async-start | bytes 2621440 | tf_op jit(solution)/shard_map/all_gather | solution.py:152
  11.9 81.7 %all-gather.12.cloned.1.call-start = ((), (), s32[]{:S(2)}) async-start(), calls=%async_computation.12 | async-start | bytes 3538944 | tf_op jit(solution)/shard_map/all_gather | solution.py:114
  12.6 409.0 %all-gather.14.cloned.1.call-start = ((), (), s32[]{:S(2)}) async-start(), calls=%async_computation.13 | async-start | bytes 1179648 | tf_op jit(solution)/shard_map/all_gather | solution.py:118
  13.4 456.4 %reduce-scatter.24.cloned.1.call-start = ((), (), s32[]{:S(2)}) async-start(), calls=%async_computation.14 | async-start | bytes 2621440 | tf_op jit(solution)/shard_map/reduce_scatter | solution.py:168
  425.8 76.8 %all-gather.18.cloned.1.call-start = ((), (), s32[]{:S(2)}) async-start(), calls=%async_computation.16 | async-start | bytes 3244032 | tf_op jit(solution)/shard_map/all_gather | solution.py:124
  426.4 124.3 %all-gather.16.cloned.1.call-start = ((), (), s32[]{:S(2)}) async-start(), calls=%async_computation.15 | async-start | bytes 2621440 | tf_op jit(solution)/shard_map/all_gather | solution.py:177
  471.2 212.5 %copy-start.87 = (f32[256]{0:T(256)}, f32[256]{0:T(256)S(1)}, u32[]{:S(2)}) copy-start(f32[256]{0:T(256)S(1)} %add_rsqrt_fusion.3) | copy-start | bytes 3076
  473.4 103.3 %all-gather.20.cloned.1.call-start = ((), (), s32[]{:S(2)}) async-start(), calls=%async_computation.17 | async-start | bytes 1622016 | tf_op jit(solution)/shard_map/all_gather | solution.py:125
  474.2 150.2 %all-gather.22.cloned.1.call-start = ((), (), s32[]{:S(2)}) async-start(), calls=%async_computation.19 | async-start | bytes 2621440 | tf_op jit(solution)/shard_map/all_gather | solution.py:191
  474.9 206.2 %reduce-scatter.28.cloned.1.call-start = ((), (), s32[]{:S(2)}) async-start(), calls=%async_computation.20 | async-start | bytes 2621440 | tf_op jit(solution)/shard_map/reduce_scatter | solution.py:199
  638.4 361.7 %all-gather.24.cloned.1.call-start = ((), (), s32[]{:S(2)}) async-start(), calls=%async_computation.21 | async-start | bytes 2621440 | tf_op jit(solution)/shard_map/all_gather | solution.py:219
  686.5 695.8 %reduce-scatter.44.cloned.1.call-start = ((), (), s32[]{:S(2)}) async-start(), calls=%async_computation.29 | async-start | bytes 1769472
  695.2 689.1 %reduce-scatter.42.cloned.1.call-start = ((), (), s32[]{:S(2)}) async-start(), calls=%async_computation.28 | async-start | bytes 3244032
  1000.1 387.5 %reduce-scatter.38.cloned.1.call-start = ((), (), s32[]{:S(2)}) async-start(), calls=%async_computation.26 | async-start | bytes 73728
  1341.8 69.6 %reduce-scatter.36.cloned.1.call-start = ((), (), s32[]{:S(2)}) async-start(), calls=%async_computation.25 | async-start | bytes 147456
  1343.2 105.6 %reduce-scatter.34.cloned.1.call-start = ((), (), s32[]{:S(2)}) async-start(), calls=%async_computation.24 | async-start | bytes 294912
  1345.2 143.3 %reduce-scatter.40.cloned.1.call-start = ((), (), s32[]{:S(2)}) async-start(), calls=%async_computation.27 | async-start | bytes 1179648
  1349.7 184.8 %reduce-scatter.30.cloned.1.call-start = ((), (), s32[]{:S(2)}) async-start(), calls=%async_computation.22 | async-start | bytes 2621440 | tf_op jit(solution)/shard_map/reduce_scatter | solution.py:236
  1369.7 211.3 %reduce-scatter.26.cloned.1.call-start = ((), (), s32[]{:S(2)}) async-start(), calls=%async_computation.18 | async-start | bytes 2621440 | tf_op jit(solution)/shard_map/reduce_scatter | solution.py:185
  1375.0 254.9 %reduce-scatter.32.cloned.1.call-start = ((), (), s32[]{:S(2)}) async-start(), calls=%async_computation.23 | async-start | bytes 3538944 | tf_op jit(solution)/shard_map/reduce_scatter | solution.py:250
  1382.2 198.8 %copy-start.18 = (bf16[256,1024]{1,0:T(8,128)(2,1)S(1)}, bf16[256,1024]{1,0:T(8,128)(2,1)}, u32[]{:S(2)}) copy-start(bf16[256,1024]{1,0:T(8,128)(2,1)} %reduce-scatter.24.cloned.1.call-done) | copy-start | bytes 1572868
  1382.2 198.8 %copy-start.29 = (bf16[256,1024]{1,0:T(8,128)(2,1)S(1)}, bf16[256,1024]{1,0:T(8,128)(2,1)}, u32[]{:S(2)}) copy-start(bf16[256,1024]{1,0:T(8,128)(2,1)} %param.21) | copy-start | bytes 1572868
  1382.2 198.8 %copy-start.30 = (bf16[256,1024]{1,0:T(8,128)(2,1)S(1)}, bf16[256,1024]{1,0:T(8,128)(2,1)}, u32[]{:S(2)}) copy-start(bf16[256,1024]{1,0:T(8,128)(2,1)} %reduce-scatter.28.cloned.1.call-done) | copy-start | bytes 1572868
  1382.2 198.8 %copy-start.88 = (f32[256]{0:T(256)S(1)}, f32[256]{0:T(256)}, u32[]{:S(2)}) copy-start(f32[256]{0:T(256)} %copy-done.87) | copy-start | bytes 3076
  (139 other events, 2738.7 us)
Sparse Core Ops, SparseCore 0:
  12.0 48.6 all-gather.9
  62.6 31.0 all-gather.11
  95.5 23.5 all-gather.13
  425.9 43.7 reduce-scatter.23
  471.6 30.9 all-gather.17
  504.7 45.9 all-gather.15
  552.7 24.0 all-gather.19
  578.4 45.9 all-gather.21
  638.6 42.5 reduce-scatter.27
  686.6 45.2 all-gather.23
  735.2 37.1 reduce-scatter.43
  1000.2 44.1 reduce-scatter.41
  1342.0 32.6 reduce-scatter.37
  1378.1 33.3 reduce-scatter.35
  1415.2 33.5 reduce-scatter.33
  1452.5 35.9 reduce-scatter.39
  1490.6 43.8 reduce-scatter.29
  1536.8 44.2 reduce-scatter.25
  1584.4 45.4 reduce-scatter.31
where the time goes:
time: 1650 us; the launch traced here: 1640 us
  waiting for transfers between devices  458 us (28%)
  other arithmetic  419 us (25%)
  matrix products  381 us (23%)
  local copies, waits for them, and re-layouts  290 us (18%)
  blocking collectives  70 us (4%)
    another operation x6, other arithmetic, delta_rule(): lax.linalg.triangular_solve(lower_mat, sides, left_side=True, lower=True,...  321 us
    unnamed x25, waiting for transfers between devices  100 us
    squeeze x96, local copies, waits for them, and re-layouts, delta_rule(): lax.scan(jax.checkpoint(block_step), state, (query_b, key_end, carried, c...  87.6 us
    dot_general x64, matrix products, block_step(): jnp.einsum('bhij,bhje->bhie', attend, deltas, precision=highest)  75.4 us
    dot_general x80, matrix products, block_step(): jnp.einsum('bhid,bhde->bhie', across, state, precision=highest)  69.5 us
    dot_general x80, matrix products, block_step(): jnp.einsum('bhid,bhde->bhie', query, state, precision=highest)  68.9 us
    dot_general x64, matrix products, block_step(): jnp.einsum('bhjd,bhje->bhde', key_end, deltas, precision=highest)  61.8 us
    all_gather x1, waiting for transfers between devices, shards(): rows_two = lax.all_gather(normed_two, 'tensor', axis=0, tiled=True)  48 us
  transfers between devices with their start and end apart: 19, of which 14 were waited for; matrix products, arithmetic and copies ran while one was open for 64% of the time, Pallas kernels for 0%

commit v1 on v0

v1 whole, which is shorter than its diff:
```python
import functools
import jax
import jax.numpy as jnp
from jax import lax
from jax.experimental import pallas as pl
from jax.experimental.pallas import tpu as pltpu
from jax.sharding import PartitionSpec as P

DK = 128
DV = 256
MIX = 2 * DK + 2 * DV
CONV = 2 * DK + DV
CHUNK = 128
LANES = 128
TAPS = 4
BETA_AT = 8

NN = ((1,), (0,))
NT = ((1,), (1,))
TN = ((0,), (0,))

f32 = jnp.float32
bf16 = jnp.bfloat16


def dot(a, b, dims, passes):
    if passes == 6:
        return lax.dot_general(
            a, b, (dims, ((), ())), precision=lax.Precision.HIGHEST, preferred_element_type=f32
        )
    a_hi = a.astype(bf16)
    b_hi = b.astype(bf16)
    out = lax.dot_general(a_hi, b_hi, (dims, ((), ())), preferred_element_type=f32)
    if passes == 3:
        a_lo = (a - a_hi.astype(f32)).astype(bf16)
        b_lo = (b - b_hi.astype(f32)).astype(bf16)
        out = out + lax.dot_general(a_hi, b_lo, (dims, ((), ())), preferred_element_type=f32)
        out = out + lax.dot_general(a_lo, b_hi, (dims, ((), ())), preferred_element_type=f32)
    return out


def exact_left(mask, b):
    hi = b.astype(bf16)
    rest = b - hi.astype(f32)
    mid = rest.astype(bf16)
    low = (rest - mid.astype(f32)).astype(bf16)
    out = lax.dot_general(mask, hi, (NN, ((), ())), preferred_element_type=f32)
    out = out + lax.dot_general(mask, mid, (NN, ((), ())), preferred_element_type=f32)
    return out + lax.dot_general(mask, low, (NN, ((), ())), preferred_element_type=f32)


def sigmoid(x):
    return 1.0 / (1.0 + jnp.exp(-x))


def log1p(y):
    return jnp.where(y < 1e-4, y - 0.5 * y * y, jnp.log(1.0 + y))


def softplus(x):
    return jnp.maximum(x, 0.0) + log1p(jnp.exp(-jnp.abs(x)))


def iotas():
    shape = (CHUNK, CHUNK)
    return lax.broadcasted_iota(jnp.int32, shape, 0), lax.broadcasted_iota(jnp.int32, shape, 1)


def token_scalars(info, head_rows, heads):
    row, col = iotas()
    beta = sigmoid(info)
    rate = -jnp.exp(head_rows[0:1])
    pre = info + head_rows[1:2]
    g = rate * softplus(pre)
    total = exact_left((row >= col).astype(bf16), g)
    lane = lax.broadcasted_iota(jnp.int32, (CHUNK, LANES), 1)
    across = jnp.where(lane < BETA_AT, info, total).T
    return beta, g, pre, total, across


def head_scalars(h, heads, info, beta, total, across):
    row, col = iotas()
    at = BETA_AT + heads + h
    seg_col = info[:, 0:1]
    seg_row = across[0:1, :]
    tot_col = total[:, at : at + 1]
    tot_row = across[at : at + 1, :]
    keep = (seg_col == seg_row) & (row >= col)
    decay = jnp.exp(jnp.where(keep, tot_col - tot_row, -1e30))
    strict = jnp.where(row > col, decay, 0.0)
    beta_col = beta[:, BETA_AT + h : BETA_AT + h + 1]
    carried = jnp.exp(tot_col) * info[:, 7:8]
    last = CHUNK - 1
    end = jnp.where(
        seg_col == seg_col[last : last + 1], jnp.exp(tot_col[last : last + 1] - tot_col), 0.0
    )
    carried_last = carried[last : last + 1]
    return decay, strict, beta_col, carried, end, carried_last


def invert(lower, passes):
    row, col = iotas()
    eye = jnp.where(row == col, 1.0, 0.0)
    size = 1
    inv = None
    while size < CHUNK:
        part = ((row // (2 * size)) == (col // (2 * size))) & ((row // size) != (col // size))
        step = jnp.where(part, lower, 0.0)
        if inv is None:
            inv = eye - step
        else:
            inv = inv - dot(inv, dot(step, inv, NN, passes), NN, passes)
        size *= 2
    return inv


def normalised(act):
    factor = lax.rsqrt(jnp.sum(act * act, -1, keepdims=True) + 1e-06)
    return act * factor, factor


def forward_body(
    heads, prec, info_ref, proj_ref, conv_ref, head_ref, onorm_ref,
    z_ref, mixed_ref, out_ref, delta_ref, across_ref, state_out_ref, solve_ref, kk_ref, qk_ref,
    state_ref, tail_ref,
):
    @pl.when(pl.program_id(0) == 0)
    def _():
        state_ref[...] = jnp.zeros_like(state_ref)
        tail_ref[...] = jnp.zeros_like(tail_ref)

    info = info_ref[...]
    beta, g, pre, total, across = token_scalars(info, head_ref[...], heads)
    for h in range(heads):
        at = h * MIX
        cat = h * CONV
        part = proj_ref[:, at : at + CONV]
        ext = jnp.concatenate([tail_ref[:, cat : cat + CONV], part], 0)
        tail_ref[:, cat : cat + CONV] = part[CHUNK - 8 :]
        mixed = conv_ref[TAPS - 1 : TAPS, cat : cat + CONV] * part
        for s in range(1, TAPS):
            shifted = ext[8 - s : 8 - s + CHUNK]
            mixed = mixed + conv_ref[TAPS - 1 - s : TAPS - s, cat : cat + CONV] * jnp.where(
                info[:, s : s + 1] > 0.5, shifted, 0.0
            )
        mixed_ref[:, cat : cat + CONV] = mixed
        act = mixed * sigmoid(mixed)
        query, _ = normalised(act[:, :DK])
        query = query * DK ** (-0.5)
        key, _ = normalised(act[:, DK : 2 * DK])
        value = act[:, 2 * DK :]
        decay, strict, beta_col, carried, end, carried_last = head_scalars(
            h, heads, info, beta, total, across
        )
        inner = dot(jnp.concatenate([key, query], 0), key, NT, prec["kk"])
        kk = inner[:CHUNK]
        qk = inner[CHUNK:]
        kk_ref[0, h] = kk
        qk_ref[0, h] = qk
        inv = invert(beta_col * strict * kk, prec["inv"])
        solve_ref[0, h] = inv
        sides = jnp.concatenate([beta_col * value, (beta_col * carried) * key], 1)
        solved = dot(inv, sides, NN, prec["solve"])
        state = state_ref[h]
        state_out_ref[0, h] = state
        reads = dot(
            jnp.concatenate([carried * query, solved[:, DV:]], 0), state, NN, prec["state"]
        )
        delta = solved[:, :DV] - reads[CHUNK:]
        result = reads[:CHUNK] + dot(decay * qk, delta, NN, prec["attend"])
        state_ref[h] = carried_last * state + dot(end * key, delta, TN, prec["state"])
        across_ref[:, h * DK : (h + 1) * DK] = solved[:, DV:]
        delta_ref[:, h * DV : (h + 1) * DV] = delta
        out_ref[:, h * DV : (h + 1) * DV] = result
        gate = proj_ref[:, at + CONV : at + MIX]
        factor = lax.rsqrt(jnp.mean(result * result, -1, keepdims=True) + 1e-05)
        z = result * factor * onorm_ref[:, h * DV : (h + 1) * DV] * (gate * sigmoid(gate))
        z_ref[:, h * DV : (h + 1) * DV] = z.astype(bf16)


def backward_body(
    heads, prec, info_ref, proj_ref, conv_ref, head_ref, onorm_ref,
    mixed_ref, out_ref, delta_ref, across_ref, state_in_ref, solve_ref, kk_ref, qk_ref, dz_ref,
    dproj_ref, dsmall_ref, dconv_ref, dhead_ref, donorm_ref,
    dstate_ref, lead_ref,
):
    @pl.when(pl.program_id(0) == 0)
    def _():
        dstate_ref[...] = jnp.zeros_like(dstate_ref)
        lead_ref[...] = jnp.zeros_like(lead_ref)
        dconv_ref[...] = jnp.zeros_like(dconv_ref)
        dhead_ref[...] = jnp.zeros_like(dhead_ref)
        donorm_ref[...] = jnp.zeros_like(donorm_ref)

    info = info_ref[...]
    beta, g, pre, total, across = token_scalars(info, head_ref[...], heads)
    row, col = iotas()
    lane = lax.broadcasted_iota(jnp.int32, (CHUNK, LANES), 1)
    dbeta_all = jnp.zeros((CHUNK, LANES), f32)
    reach_all = jnp.zeros((CHUNK, LANES), f32)
    leave_all = jnp.zeros((CHUNK, LANES), f32)
    spans_all = jnp.zeros((CHUNK, LANES), f32)
    from_here = (row <= col).astype(bf16)
    for h in range(heads):
        at = h * MIX
        cat = h * CONV
        mixed = mixed_ref[:, cat : cat + CONV]
        msig = sigmoid(mixed)
        act = mixed * msig
        q_unit, q_factor = normalised(act[:, :DK])
        query = q_unit * DK ** (-0.5)
        key, k_factor = normalised(act[:, DK : 2 * DK])
        value = act[:, 2 * DK :]
        decay, strict, beta_col, carried, end, carried_last = head_scalars(
            h, heads, info, beta, total, across
        )
        kk = kk_ref[0, h]
        qk = qk_ref[0, h]
        inv = solve_ref[0, h]
        delta = delta_ref[:, h * DV : (h + 1) * DV]
        across_w = across_ref[:, h * DK : (h + 1) * DK]
        result = out_ref[:, h * DV : (h + 1) * DV]
        state = state_in_ref[0, h]
        dnext = dstate_ref[h]
        gate = proj_ref[:, at + CONV : at + MIX]
        gsig = sigmoid(gate)
        silu = gate * gsig
        onorm = onorm_ref[:, h * DV : (h + 1) * DV]
        factor = lax.rsqrt(jnp.mean(result * result, -1, keepdims=True) + 1e-05)
        normed = result * factor
        dz = dz_ref[:, h * DV : (h + 1) * DV].astype(f32)
        dzn = dz * normed
        donorm_ref[:, h * DV : (h + 1) * DV] += jnp.sum(dzn * silu, 0, keepdims=True)
        dgate = dzn * onorm * (gsig * (1.0 + gate * (1.0 - gsig)))
        dproj_ref[:, at + CONV : at + MIX] = dgate.astype(bf16)
        dnormed = dz * onorm * silu
        dout = factor * (dnormed - normed * jnp.mean(dnormed * normed, -1, keepdims=True))
        ends = end * key
        ddelta = dot(decay * qk, dout, TN, prec["attend"]) + dot(ends, dnext, NN, prec["state"])
        dstate_ref[h] = carried_last * dnext + dot(
            jnp.concatenate([carried * query, -across_w], 0),
            jnp.concatenate([dout, ddelta], 0),
            TN,
            prec["state"],
        )
        x = dot(inv, ddelta, TN, prec["solve"])
        big = dot(
            jnp.concatenate([dout, x], 0), jnp.concatenate([state, delta], 0), NT, prec["big"]
        )
        dqc = big[:CHUNK, :DK]
        dp = big[:CHUNK, DK:]
        dkb = -big[CHUNK:, :DK]
        dm = -big[CHUNK:, DK:]
        dend = dot(delta, dnext, NT, prec["big"])
        dcl = jnp.sum(jnp.sum(state * dnext, 0, keepdims=True), 1, keepdims=True)
        dqk = decay * dp
        das = strict * dm
        rows = dot(jnp.concatenate([dqk, das], 0), key, NN, prec["kk"])
        dq = rows[:CHUNK] + carried * dqc
        das_k = rows[CHUNK:]
        bdas = beta_col * das
        cols = dot(
            jnp.concatenate([dqk, bdas], 0),
            jnp.concatenate([query, key], 0),
            TN,
            prec["kk"],
        )
        dk_end = end * dend
        dkb_c = carried * dkb
        dk_row_b = das_k + dkb_c
        dk = beta_col * dk_row_b + cols + dk_end
        xv = x * value
        dbeta = jnp.sum(xv[:, :DK] + xv[:, DK:] + key * dk_row_b, -1, keepdims=True)
        reach = jnp.sum(query * (carried * dqc) + key * (beta_col * dkb_c), -1, keepdims=True)
        leave = jnp.sum(key * dk_end, -1, keepdims=True)
        pairs = jnp.where(row > col, dqk * qk + bdas * kk, 0.0)
        pairs = exact_left(from_here, pairs)
        spans = jnp.sum(jnp.where(row > col, pairs, 0.0), -1, keepdims=True) + carried_last * dcl
        dbeta_all = jnp.where(lane == BETA_AT + h, dbeta, dbeta_all)
        at_h = lane == BETA_AT + heads + h
        reach_all = jnp.where(at_h, reach, reach_all)
        leave_all = jnp.where(at_h, leave, leave_all)
        spans_all = jnp.where(at_h, spans, spans_all)
        dv = beta_col * x
        scale_q = DK ** (-0.5) * q_factor
        daq = scale_q * (dq - q_unit * jnp.sum(q_unit * dq, -1, keepdims=True))
        dak = k_factor * (dk - key * jnp.sum(key * dk, -1, keepdims=True))
        dact = jnp.concatenate([daq, dak, dv], 1)
        dmixed = dact * (msig * (1.0 + mixed * (1.0 - msig)))
        ext = jnp.concatenate([dmixed, lead_ref[:, cat : cat + CONV]], 0)
        lead_ref[:, cat : cat + CONV] = dmixed[:8]
        part = proj_ref[:, at : at + CONV]
        dpart = conv_ref[TAPS - 1 : TAPS, cat : cat + CONV] * dmixed
        dconv_ref[TAPS - 1 : TAPS, cat : cat + CONV] += jnp.sum(dmixed * part, 0, keepdims=True)
        for s in range(1, TAPS):
            shifted = jnp.where(info[:, 3 + s : 4 + s] > 0.5, ext[s : s + CHUNK], 0.0)
            dpart = dpart + conv_ref[TAPS - 1 - s : TAPS - s, cat : cat + CONV] * shifted
            dconv_ref[TAPS - 1 - s : TAPS - s, cat : cat + CONV] += jnp.sum(
                shifted * part, 0, keepdims=True
            )
        dproj_ref[:, at : at + CONV] = dpart.astype(bf16)
    dg = spans_all + exact_left(from_here, reach_all)
    dg = dg + exact_left((row > col).astype(bf16), leave_all)
    rate = -jnp.exp(head_ref[0:1])
    dpre = dg * rate * sigmoid(pre)
    dsmall_ref[...] = dbeta_all * beta * (1.0 - beta) + dpre
    dhead_ref[0:1] += jnp.sum(dg * g, 0, keepdims=True)
    dhead_ref[1:2] += jnp.sum(dpre, 0, keepdims=True)


PREC = {"kk": 3, "inv": 3, "solve": 3, "state": 3, "attend": 3, "big": 3}
BUDGET = 56 << 20


def mixer_forward(info, proj, conv, head_rows, onorm, heads, prec=PREC):
    length = proj.shape[0]
    count = length // CHUNK
    chunk = lambda width: pl.BlockSpec((CHUNK, width), lambda c: (c, 0))
    whole = lambda rows, width: pl.BlockSpec((rows, width), lambda c: (0, 0))
    square = lambda rows, width: pl.BlockSpec((1, heads, rows, width), lambda c: (c, 0, 0, 0))
    return pl.pallas_call(
        functools.partial(forward_body, heads, prec),
        grid=(count,),
        in_specs=[
            chunk(LANES), chunk(heads * MIX), whole(TAPS, heads * CONV), whole(8, LANES),
            whole(1, heads * DV),
        ],
        out_specs=[
            chunk(heads * DV), chunk(heads * CONV), chunk(heads * DV), chunk(heads * DV),
            chunk(heads * DK), square(DK, DV), square(CHUNK, CHUNK), square(CHUNK, CHUNK),
            square(CHUNK, CHUNK),
        ],
        out_shape=[
            jax.ShapeDtypeStruct((length, heads * DV), bf16),
            jax.ShapeDtypeStruct((length, heads * CONV), f32),
            jax.ShapeDtypeStruct((length, heads * DV), f32),
            jax.ShapeDtypeStruct((length, heads * DV), f32),
            jax.ShapeDtypeStruct((length, heads * DK), f32),
            jax.ShapeDtypeStruct((count, heads, DK, DV), f32),
            jax.ShapeDtypeStruct((count, heads, CHUNK, CHUNK), f32),
            jax.ShapeDtypeStruct((count, heads, CHUNK, CHUNK), f32),
            jax.ShapeDtypeStruct((count, heads, CHUNK, CHUNK), f32),
        ],
        scratch_shapes=[
            pltpu.VMEM((heads, DK, DV), f32),
            pltpu.VMEM((8, heads * CONV), f32),
        ],
        compiler_params=pltpu.CompilerParams(
            dimension_semantics=("arbitrary",), vmem_limit_bytes=BUDGET
        ),
        name="mixer_forward",
    )(info, proj, conv, head_rows, onorm)


def mixer_backward(info, proj, conv, head_rows, onorm, kept, dz, heads, prec=PREC):
    length = proj.shape[0]
    count = length // CHUNK
    chunk = lambda width: pl.BlockSpec((CHUNK, width), lambda c: (count - 1 - c, 0))
    whole = lambda rows, width: pl.BlockSpec((rows, width), lambda c: (0, 0))
    square = lambda rows, width: pl.BlockSpec(
        (1, heads, rows, width), lambda c: (count - 1 - c, 0, 0, 0)
    )
    return pl.pallas_call(
        functools.partial(backward_body, heads, prec),
        grid=(count,),
        in_specs=[
            chunk(LANES), chunk(heads * MIX), whole(TAPS, heads * CONV), whole(8, LANES),
            whole(1, heads * DV),
            chunk(heads * CONV), chunk(heads * DV), chunk(heads * DV),
            chunk(heads * DK), square(DK, DV), square(CHUNK, CHUNK), square(CHUNK, CHUNK),
            square(CHUNK, CHUNK), chunk(heads * DV),
        ],
        out_specs=[
            chunk(heads * MIX), chunk(LANES), whole(TAPS, heads * CONV), whole(8, LANES),
            whole(1, heads * DV),
        ],
        out_shape=[
            jax.ShapeDtypeStruct((length, heads * MIX), bf16),
            jax.ShapeDtypeStruct((length, LANES), f32),
            jax.ShapeDtypeStruct((TAPS, heads * CONV), f32),
            jax.ShapeDtypeStruct((8, LANES), f32),
            jax.ShapeDtypeStruct((1, heads * DV), f32),
        ],
        scratch_shapes=[
            pltpu.VMEM((heads, DK, DV), f32),
            pltpu.VMEM((8, heads * CONV), f32),
        ],
        compiler_params=pltpu.CompilerParams(
            dimension_semantics=("arbitrary",), vmem_limit_bytes=BUDGET
        ),
        name="mixer_backward",
    )(info, proj, conv, head_rows, onorm, *kept, dz)


def token_info(segments, small):
    length = segments.shape[-1]
    seg = segments.reshape(length)
    heads = small.shape[-1]
    columns = [seg.astype(f32)]
    for s in range(1, TAPS):
        before = jnp.concatenate([jnp.full((s,), -1, seg.dtype), seg[:-s]])
        columns.append((before == seg).astype(f32))
    for s in range(1, TAPS):
        after = jnp.concatenate([seg[s:], jnp.full((s,), -1, seg.dtype)])
        columns.append((after == seg).astype(f32))
    ends = seg.reshape(-1, CHUNK)[:, -1]
    ends = jnp.concatenate([jnp.full((1,), -1, seg.dtype), ends[:-1]])
    columns.append((jnp.repeat(ends, CHUNK) == seg).astype(f32))
    info = jnp.stack(columns, 1)
    info = jnp.concatenate([info, small.reshape(length, 2 * heads)], 1)
    return jnp.pad(info, ((0, 0), (0, LANES - BETA_AT - 2 * heads)))


def head_lanes(head):
    heads = head.shape[1]
    return jnp.pad(head, ((0, 6), (BETA_AT + heads, LANES - BETA_AT - 2 * heads)))


def norm_factor(values):
    return lax.rsqrt(jnp.mean(values * values, -1, keepdims=True) + 1e-06)


def norm_backward(grad_out, scaled, factor, gain):
    grad_scaled = grad_out * gain
    grad_input = factor * (grad_scaled - scaled * jnp.mean(grad_scaled * scaled, -1, keepdims=True))
    return (grad_input, jnp.sum(grad_out * scaled, 0))


def product(left, right, dims):
    return lax.dot_general(left, right, (dims, ((), ())), preferred_element_type=f32)


def shards(
    tokens, cotangent, segments, norm_gains, mixer_in, mixer_small, conv_weight, head_params,
    out_norm, mixer_out, ffn_in, ffn_out,
):
    heads = mixer_in.shape[1] // MIX
    all_heads = head_params.shape[1]
    head_start = lax.axis_index("tensor") * heads
    head_local = lax.dynamic_slice_in_dim(head_params, head_start, heads, 1)
    gains = norm_gains.astype(f32)
    inputs = tokens.astype(f32)
    factor_one = norm_factor(inputs)
    scaled_one = inputs * factor_one
    normed_one = (scaled_one * gains[0]).astype(bf16)
    rows_one = lax.all_gather(normed_one, "tensor", axis=0, tiled=True)
    small_shapes = [mixer_small.shape, conv_weight.shape, out_norm.shape]
    small_dims = [1, 2, 1]
    packed = jnp.concatenate([mixer_small.reshape(-1), conv_weight.reshape(-1), out_norm.reshape(-1)])
    gathered = lax.all_gather(packed, "dp", axis=0, tiled=False)
    ways = gathered.shape[0]
    pieces = []
    offset = 0
    for shape, dim in zip(small_shapes, small_dims):
        size = 1
        for extent in shape:
            size *= extent
        piece = gathered[:, offset : offset + size].reshape((ways,) + shape)
        piece = jnp.moveaxis(piece, 0, dim)
        pieces.append(
            piece.reshape(shape[:dim] + (ways * shape[dim],) + shape[dim + 1 :])
        )
        offset += size
    w_small, w_conv, w_onorm = pieces
    w_in = lax.all_gather(mixer_in, "dp", axis=0, tiled=True)
    w_out = lax.all_gather(mixer_out, "dp", axis=1, tiled=True)
    group = rows_one.shape[0]
    proj = product(rows_one, w_in, NN)
    small = jnp.einsum("nd,cdh->nch", rows_one, w_small, preferred_element_type=f32)
    info = token_info(segments, small)
    conv_rows = w_conv.astype(f32).reshape(TAPS, heads * CONV)
    onorm_row = w_onorm.astype(f32).reshape(1, heads * DV)
    head_rows = head_lanes(head_local)
    mixed, *kept = mixer_forward(info, proj, conv_rows, head_rows, onorm_row, heads)
    middle = inputs + lax.psum_scatter(
        product(mixed, w_out, NN).astype(bf16), "tensor", scatter_dimension=0, tiled=True
    ).astype(f32)
    factor_two = norm_factor(middle)
    scaled_two = middle * factor_two
    normed_two = (scaled_two * gains[1]).astype(bf16)
    rows_two = lax.all_gather(normed_two, "tensor", axis=0, tiled=True)
    w_ffn = lax.all_gather(ffn_in, "dp", axis=1, tiled=True)
    w_down = lax.all_gather(ffn_out, "dp", axis=1, tiled=True)
    grad_rows = lax.all_gather(cotangent, "tensor", axis=0, tiled=True)
    gate_part = product(rows_two, w_ffn[0], NN)
    up_part = product(rows_two, w_ffn[1], NN)
    sigma = jax.nn.sigmoid(gate_part)
    activ = gate_part * sigma
    hidden = (activ * up_part).astype(bf16)
    result = middle + lax.psum_scatter(
        product(hidden, w_down, NN).astype(bf16), "tensor", scatter_dimension=0, tiled=True
    ).astype(f32)
    grad_hidden = product(grad_rows, w_down, NT)
    grad_down = product(hidden, grad_rows, TN)
    grad_gate = (grad_hidden * up_part * sigma * (1.0 + gate_part * (1.0 - sigma))).astype(bf16)
    grad_up = (grad_hidden * activ).astype(bf16)
    grad_normed_two = lax.psum_scatter(
        (product(grad_gate, w_ffn[0], NT) + product(grad_up, w_ffn[1], NT)).astype(bf16),
        "tensor",
        scatter_dimension=0,
        tiled=True,
    ).astype(f32)
    grad_ffn = jnp.stack([product(rows_two, grad_gate, TN), product(rows_two, grad_up, TN)])
    grad_middle_norm, grad_gain_two = norm_backward(
        grad_normed_two, scaled_two, factor_two, gains[1]
    )
    grad_middle = cotangent.astype(f32) + grad_middle_norm
    out_ffn = lax.psum_scatter(grad_ffn.astype(bf16), "dp", scatter_dimension=1, tiled=True)
    out_down = lax.psum_scatter(grad_down.astype(bf16), "dp", scatter_dimension=1, tiled=True)
    branch_grad = lax.all_gather(grad_middle.astype(bf16), "tensor", axis=0, tiled=True)
    grad_mixed = product(branch_grad, w_out, NT)
    grad_out = product(mixed, branch_grad, TN)
    grad_proj, grad_info, grad_conv, grad_head, grad_onorm = mixer_backward(
        info, proj, conv_rows, head_rows, onorm_row, kept, grad_mixed, heads
    )
    grad_small = grad_info[:, BETA_AT : BETA_AT + 2 * heads].reshape(group, 2, heads).astype(bf16)
    grad_normed_one = product(grad_proj, w_in, NT) + jnp.einsum(
        "nch,cdh->nd", grad_small, w_small, preferred_element_type=f32
    )
    grad_gain_one = jnp.sum(grad_normed_one * rows_one.astype(f32), 0) / gains[0]
    grad_normed_one = lax.psum_scatter(
        grad_normed_one.astype(bf16), "tensor", scatter_dimension=0, tiled=True
    ).astype(f32)
    grad_in = product(rows_one, grad_proj, TN)
    grad_small_w = jnp.einsum("nd,nch->cdh", rows_one, grad_small, preferred_element_type=f32)
    head_full = lax.dynamic_update_slice_in_dim(
        jnp.zeros((2, all_heads), f32),
        grad_head[:2, BETA_AT + heads : BETA_AT + 2 * heads],
        head_start,
        1,
    )
    gain_total, head_total = lax.psum(
        (jnp.stack([grad_gain_one, grad_gain_two]), head_full), ("dp", "tensor")
    )
    grad_scaled = grad_normed_one * gains[0]
    grad_tokens = grad_middle + factor_one * (
        grad_scaled - scaled_one * jnp.mean(grad_scaled * scaled_one, -1, keepdims=True)
    )
    out_in = lax.psum_scatter(grad_in.astype(bf16), "dp", scatter_dimension=0, tiled=True)
    out_out = lax.psum_scatter(grad_out.astype(bf16), "dp", scatter_dimension=1, tiled=True)
    smalls = [
        grad_small_w,
        grad_conv.reshape(TAPS, heads, CONV),
        grad_onorm.reshape(heads, DV),
    ]
    flat = []
    for value, dim in zip(smalls, small_dims):
        shape = value.shape
        value = value.reshape(shape[:dim] + (ways, shape[dim] // ways) + shape[dim + 1 :])
        flat.append(jnp.moveaxis(value, dim, 0).reshape(ways, -1))
    flat = lax.psum_scatter(
        jnp.concatenate(flat, 1).astype(bf16), "dp", scatter_dimension=0, tiled=False
    ).astype(f32)
    outs = []
    offset = 0
    for shape in small_shapes:
        size = 1
        for extent in shape:
            size *= extent
        outs.append(flat[offset : offset + size].reshape(shape))
        offset += size
    return (
        result.astype(bf16),
        grad_tokens,
        gain_total,
        out_in.astype(f32),
        outs[0],
        outs[1],
        head_total,
        outs[2],
        out_out.astype(f32),
        out_ffn.astype(f32),
        out_down.astype(f32),
    )


def solution(mesh):
    in_specs = (
        P(("dp", "tensor"), None),
        P(("dp", "tensor"), None),
        P("dp", None),
        P(),
        P("dp", "tensor"),
        P(None, "dp", "tensor"),
        P(None, "tensor", "dp"),
        P(),
        P("tensor", "dp"),
        P("tensor", "dp"),
        P(None, "dp", "tensor"),
        P("tensor", "dp"),
    )
    out_specs = (
        P(("dp", "tensor"), None),
        P(("dp", "tensor"), None),
        P(),
        P("dp", "tensor"),
        P(None, "dp", "tensor"),
        P(None, "tensor", "dp"),
        P(),
        P("tensor", "dp"),
        P("tensor", "dp"),
        P(None, "dp", "tensor"),
        P("tensor", "dp"),
    )
    return jax.shard_map(shards, mesh=mesh, in_specs=in_specs, out_specs=out_specs, check_vma=False)
```

time: 1650 us -> 749 us (0.45)
  other arithmetic: 419 us -> 25.6 us
  matrix products: 381 us -> 76.1 us
  local copies, waits for them, and re-layouts: 290 us -> 38.2 us
  Pallas kernels: 0 us -> 82.5 us
  waiting for transfers between devices: 458 us -> 398 us
  blocking collectives: 70 us -> 96.4 us
    another operation x24 -> x4, other arithmetic: 322 us -> 1.92 us  [the longest x1 1.82 us: shards(): jnp.stack([product(rows_two, grad_gate, TN), product(rows_two, grad_up, T...]
    dot_general x310 -> x18, matrix products: 372 us -> 76.1 us  [the longest x15 70.5 us: product(): lax.dot_general(left, right, (dims, ((), ())), preferred_element_type=f32)]
    squeeze x97 -> x0, local copies, waits for them, and re-layouts: 87.7 us -> none  [the longest x96 87.6 us: delta_rule(): lax.scan(jax.checkpoint(block_step), state, (query_b, key_end, carried, c...]
    unnamed x25 -> x19, waiting for transfers between devices: 100 us -> 16 us
    pallas_call x0 -> x2, Pallas kernels: none -> 82.5 us  [the longest x1 52.3 us: mixer_forward(): pl.pallas_call(functools.partial(forward_body, heads, prec), grid=(count,...]
    unnamed x0 -> x2, blocking collectives: none -> 53.6 us
    mul x66 -> x0, local copies, waits for them, and re-layouts: 42.7 us -> none  [the longest x32 21.2 us: block_step(): carried[..., None]]
    dynamic_slice x65 -> x1, local copies, waits for them, and re-layouts: 42.6 us -> 0.07 us  [shards(): head_local = lax.dynamic_slice_in_dim(head_params, head_start, heads, 1)]
  transfers between devices with their start and end apart: 19 -> 16, of which waited for: 14 -> 13; matrix products, arithmetic and copies ran while one was open for 64% -> 15% of each run, Pallas kernels for 0% -> 11%
where the time goes in v1:
time: 749 us; the launch traced here: 741 us
  waiting for transfers between devices  398 us (53%)
  blocking collectives  96.4 us (13%)
  Pallas kernels  82.5 us (11%)
  matrix products  76.1 us (10%)
  local copies, waits for them, and re-layouts  38.2 us (5%)
  other arithmetic  25.6 us (3%)
  between operations  15.4 us (2%)
  starting transfers between devices  9.57 us (1%)
    dot_general x15, matrix products, product(): lax.dot_general(left, right, (dims, ((), ())), preferred_element_type=f32)  70.5 us
    unnamed x2, blocking collectives  53.6 us
    pallas_call x1, Pallas kernels, mixer_forward(): pl.pallas_call(functools.partial(forward_body, heads, prec), grid=(count,...  52.3 us
    all_gather x1, waiting for transfers between devices, shards(): rows_two = lax.all_gather(normed_two, 'tensor', axis=0, tiled=True)  48 us
    all_gather x1, waiting for transfers between devices, shards(): grad_rows = lax.all_gather(cotangent, 'tensor', axis=0, tiled=True)  47.6 us
    reduce_scatter x1, waiting for transfers between devices, shards(): lax.psum_scatter(grad_in.astype(bf16), 'dp', scatter_dimension=0, tiled=T...  46 us
    reduce_scatter x1, waiting for transfers between devices, shards(): lax.psum_scatter(product(hidden, w_down, NN).astype(bf16), 'tensor', scat...  44.1 us
    reduce_scatter x1, waiting for transfers between devices, shards(): lax.psum_scatter(product(mixed, w_out, NN).astype(bf16), 'tensor', scatte...  43.4 us
  transfers between devices with their start and end apart: 16, of which 13 were waited for; matrix products, arithmetic and copies ran while one was open for 15% of the time, Pallas kernels for 11%

profile of v1, /device:TPU:0, one launch (start us, length us, event | category | flops | bytes accessed | tf_op | source)
XLA Modules:
  0.0 741.3 jit_solution(5572241666086287179)
XLA Ops:
  15.2 26.7 %all-reduce.6 = bf16[8704]{0:T(1024)(128)(2,1)S(1)} all-reduce(bf16[8704]{0:T(1024)(128)(2,1)S(1)} %dynamic-update-slice), channel_id=2, replica_groups=mesh['dp'=8,'tensor'=4] {'dp'}, use_global_device_ids=true, to_apply=%add.6 | all-reduce | flops 8704 | bytes 34816
  45.1 15.1 %all-gather.10.cloned.1.call-done = bf16[1024,1024]{1,0:T(8,128)(2,1)} async-done(((bf16[256,1024]{1,0:T(8,128)(2,1)}), bf16[1024,1024]{1,0:T(8,128)(2,1)}) %all-gather.10.cloned.1.call-update) | async-done | bytes 2097168 | tf_op jit(solution)/shard_map/all_gather | solution.py:446
  63.7 29.4 %all-gather.12.cloned.1.call-done = bf16[1024,1536]{1,0:T(8,128)(2,1)} async-done(((bf16[128,1536]{1,0:T(8,128)(2,1)}), bf16[1024,1536]{1,0:T(8,128)(2,1)}) %all-gather.12.cloned.1.call-update) | async-done | bytes 3145744 | tf_op jit(solution)/shard_map/all_gather | solution.py:465
  93.1 7.2 fusion.40.proj_ref
  100.3 52.3 %mixer_forward.1 = (bf16[1024,512]{1,0:T(8,128)(2,1)}, f32[1024,1024]{1,0:T(8,128)}, f32[1024,512]{1,0:T(8,128)}, f32[1024,512]{1,0:T(8,128)}, f32[1024,256]{1,0...) custom-call(f32[1024,128]{1,0:T(8,128)} %pad.12.info_ref, ...), custom_call_target="tpu_custom_call" | custom-call | tf_op jit(solution)/shard_map/mixer_forward/pallas_call | solution.py:321
  157.4 43.4 %reduce-scatter.16.cloned.1.call-done = bf16[256,1024]{1,0:T(8,128)(2,1)} async-done(((bf16[1024,1024]{1,0:T(8,128)(2,1)}), bf16[256,1024]{1,0:T(8,128)(2,1)}) %reduce-scatter.16.cloned.1.call-update) | async-done | bytes 524304 | tf_op jit(solution)/shard_map/reduce_scatter | solution.py:475
  206.0 27.7 %all-gather.18.cloned.1.call-done = bf16[2,1024,704]{1,2,0:T(8,128)(2,1)} async-done(((bf16[2,128,704]{1,2,0:T(8,128)(2,1)}), bf16[2,1024,704]{1,2,0:T(8,128)(2,1)}) %all-gather.18.cloned.1.call-update) | async-done | bytes 2883600 | tf_op jit(solution)/shard_map/all_gather | solution.py:482
  233.7 48.0 %all-gather.16.cloned.1.call-done = bf16[1024,1024]{1,0:T(8,128)(2,1)} async-done(((bf16[256,1024]{1,0:T(8,128)(2,1)}), bf16[1024,1024]{1,0:T(8,128)(2,1)}) %all-gather.16.cloned.1.call-update) | async-done | bytes 2097168 | tf_op jit(solution)/shard_map/all_gather | solution.py:481
  290.5 17.4 %all-gather.20.cloned.1.call-done = bf16[704,1024]{1,0:T(8,128)(2,1)} async-done(((bf16[704,128]{1,0:T(8,128)(2,1)}), bf16[704,1024]{1,0:T(8,128)(2,1)}) %all-gather.20.cloned.1.call-update) | async-done | bytes 1441808 | tf_op jit(solution)/shard_map/all_gather | solution.py:483
  307.8 47.6 %all-gather.22.cloned.1.call-done = bf16[1024,1024]{1,0:T(8,128)(2,1)} async-done(((bf16[256,1024]{1,0:T(8,128)(2,1)}), bf16[1024,1024]{1,0:T(8,128)(2,1)}) %all-gather.22.cloned.1.call-update) | async-done | bytes 2097168 | tf_op jit(solution)/shard_map/all_gather | solution.py:484
  355.4 7.7 %multiply_convert_fusion = (bf16[1024,704]{0,1:T(8,128)(2,1)S(1)}, bf16[1024,704]{0,1:T(8,128)(2,1)S(1)}, bf16[1024,704]{0,1:T(8,128)(2,1)}) fusion(f32[1024,704]{0,1:T(8,128)} %fusion.9, f32[1024,704]{0,1:T(8,128)} %fusion.10, bf16[1024,1024]{1,0:T(8,128)(2,1)} %all-gather.22.cloned.1.call-done, bf16[704,1024]{1,0:T(8,128)(2,1)} %all-gather.20.cloned.1.call-done), kind=kOutput, calls=%fused_computation.5 | convolution fusion | flops 1487208448 | bytes 13631488 | tf_op jit(solution)/shard_map/dot_general | solution.py:430
  368.4 42.7 %reduce-scatter.20.cloned.1.call-done = bf16[256,1024]{1,0:T(8,128)(2,1)} async-done(((bf16[1024,1024]{1,0:T(8,128)(2,1)}), bf16[256,1024]{1,0:T(8,128)(2,1)}) %reduce-scatter.20.cloned.1.call-update) | async-done | bytes 524304 | tf_op jit(solution)/shard_map/reduce_scatter | solution.py:497
  430.7 8.7 %copy.118 = bf16[2,1024,704]{2,0,1:T(2,128)(2,1)} copy(bf16[2,1024,704]{1,2,0:T(8,128)(2,1)} %pad_maximum_fusion) | data formatting | bytes 5767168
  439.4 7.6 %reshape.279 = bf16[1024,1408]{1,0:T(8,128)(2,1)} reshape(bf16[1024,2,704]{2,1,0:T(2,128)(2,1)} %bitcast.113) | data formatting | bytes 5767168
  447.2 14.0 %all-gather.24.cloned.1.call-done = bf16[1024,1024]{1,0:T(8,128)(2,1)} async-done(((bf16[256,1024]{1,0:T(8,128)(2,1)}), bf16[1024,1024]{1,0:T(8,128)(2,1)}) %all-gather.24.cloned.1.call-update) | async-done | bytes 2097168 | tf_op jit(solution)/shard_map/all_gather | solution.py:510
  467.7 8.7 %reduce-scatter.22.cloned.1.call-start = ((), (), s32[]{:S(2)}) async-start(), calls=%async_computation.19 | async-start | bytes 2621440 | tf_op jit(solution)/shard_map/reduce_scatter | solution.py:521
  480.9 30.2 %mixer_backward.1 = (bf16[1024,1536]{1,0:T(8,128)(2,1)}, f32[1024,128]{1,0:T(8,128)}, f32[4,1024]{1,0:T(4,128)}, f32[8,128]{1,0:T(8,128)}, f32[1,512]{1,0:T(1,128)}) custom-call(f32[1024,128]{1,0:T(8,128)} %pad.12.info_ref, f32[1024,1536]{1,0:T(8,128)} %fusion.40.proj_ref, f32[4,1024]{1,0:T(4,128)} %reshape.262.conv_ref, f32[8,128]{1,0:T(8,128)} %pad.13.head_ref, ...), custom_call_target="tpu_custom_call" | custom-call | tf_op jit(solution)/shard_map/mixer_backward/pallas_call | solution.py:363
  512.5 6.7 fusion.42
  527.3 6.8 convolution_convert_fusion
  537.3 12.5 %reduce-scatter.28.cloned.1.call-done = bf16[128,1408]{1,0:T(8,128)(2,1)} async-done(((bf16[1024,1408]{1,0:T(8,128)(2,1)}), bf16[128,1408]{1,0:T(8,128)(2,1)}) %reduce-scatter.28.cloned.1.call-update) | async-done | bytes 360464
  555.4 26.9 %all-reduce.7 = bf16[8,1088]{0,1:T(8,128)(2,1)S(1)} all-reduce(bf16[8,1088]{0,1:T(8,128)(2,1)S(1)} %pad_maximum_fusion.1), channel_id=8, replica_groups=mesh['dp'=8,'tensor'=4] {'dp'}, use_global_device_ids=true, to_apply=%region_12.13.clone | all-reduce | flops 8704 | bytes 34816
  587.2 42.8 %all-reduce.8 = (f32[2,1024]{1,0:T(2,128)}, f32[2,8]{1,0:T(2,128)}) all-reduce(f32[2,1024]{1,0:T(2,128)S(1)} %pad_maximum_fusion.2, f32[2,8]{1,0:T(2,128)S(1)} %dynamic_update_slice.3), channel_id=1, replica_groups=mesh['dp'=8,'tensor'=4] {'dp','tensor'}, use_global_device_ids=true, to_apply=%region_10.11 | all-reduce | flops 2064 | bytes 16512 | tf_op jit(solution)/shard_map/psum | solution.py:532
  639.3 44.1 %reduce-scatter.18.cloned.1.call-done = bf16[256,1024]{1,0:T(8,128)(2,1)} async-done(((bf16[1024,1024]{1,0:T(8,128)(2,1)}), bf16[256,1024]{1,0:T(8,128)(2,1)}) %reduce-scatter.18.cloned.1.call-update) | async-done | bytes 524304 | tf_op jit(solution)/shard_map/reduce_scatter | solution.py:490
  686.5 46.0 %reduce-scatter.24.cloned.1.call-done = bf16[128,1536]{1,0:T(8,128)(2,1)} async-done(((bf16[1024,1536]{1,0:T(8,128)(2,1)}), bf16[128,1536]{1,0:T(8,128)(2,1)}) %reduce-scatter.24.cloned.1.call-update) | async-done | bytes 393232 | tf_op jit(solution)/shard_map/reduce_scatter | solution.py:539
  (200 shorter events, 105.7 us)
Async XLA Ops:
  7.2 52.9 %all-gather.10.cloned.1.call-start = ((), (), s32[]{:S(2)}) async-start(), calls=%async_computation.8 | async-start | bytes 2621440 | tf_op jit(solution)/shard_map/all_gather | solution.py:446
  11.4 81.7 %all-gather.12.cloned.1.call-start = ((), (), s32[]{:S(2)}) async-start(), calls=%async_computation.9 | async-start | bytes 3538944 | tf_op jit(solution)/shard_map/all_gather | solution.py:465
  12.1 140.5 %all-gather.14.cloned.1.call-start = ((), (), s32[]{:S(2)}) async-start(), calls=%async_computation.10 | async-start | bytes 1179648 | tf_op jit(solution)/shard_map/all_gather | solution.py:466
  12.9 188.0 %reduce-scatter.16.cloned.1.call-start = ((), (), s32[]{:S(2)}) async-start(), calls=%async_computation.11 | async-start | bytes 2621440 | tf_op jit(solution)/shard_map/reduce_scatter | solution.py:475
  156.8 76.9 %all-gather.18.cloned.1.call-start = ((), (), s32[]{:S(2)}) async-start(), calls=%async_computation.13 | async-start | bytes 3244032 | tf_op jit(solution)/shard_map/all_gather | solution.py:482
  157.4 124.4 %all-gather.16.cloned.1.call-start = ((), (), s32[]{:S(2)}) async-start(), calls=%async_computation.12 | async-start | bytes 2621440 | tf_op jit(solution)/shard_map/all_gather | solution.py:481
  202.1 211.1 %copy-start.11 = (f32[256]{0:T(256)}, f32[256]{0:T(256)S(1)}, u32[]{:S(2)}) copy-start(f32[256]{0:T(256)S(1)} %add_rsqrt_fusion) | copy-start | bytes 3076
  204.2 103.6 %all-gather.20.cloned.1.call-start = ((), (), s32[]{:S(2)}) async-start(), calls=%async_computation.14 | async-start | bytes 1622016 | tf_op jit(solution)/shard_map/all_gather | solution.py:483
  205.0 150.5 %all-gather.22.cloned.1.call-start = ((), (), s32[]{:S(2)}) async-start(), calls=%async_computation.16 | async-start | bytes 2621440 | tf_op jit(solution)/shard_map/all_gather | solution.py:484
  205.7 205.3 %reduce-scatter.20.cloned.1.call-start = ((), (), s32[]{:S(2)}) async-start(), calls=%async_computation.17 | async-start | bytes 2621440 | tf_op jit(solution)/shard_map/reduce_scatter | solution.py:497
  368.3 92.8 %all-gather.24.cloned.1.call-start = ((), (), s32[]{:S(2)}) async-start(), calls=%async_computation.18 | async-start | bytes 2621440 | tf_op jit(solution)/shard_map/all_gather | solution.py:510
  415.7 119.7 %reduce-scatter.30.cloned.1.call-start = ((), (), s32[]{:S(2)}) async-start(), calls=%async_computation.23 | async-start | bytes 1769472
  423.2 126.6 %reduce-scatter.28.cloned.1.call-start = ((), (), s32[]{:S(2)}) async-start(), calls=%async_computation.22 | async-start | bytes 3244032
  447.1 182.9 %reduce-scatter.26.cloned.1.call-start = ((), (), s32[]{:S(2)}) async-start(), calls=%async_computation.21 | async-start | bytes 1179648
  467.7 170.2 %reduce-scatter.22.cloned.1.call-start = ((), (), s32[]{:S(2)}) async-start(), calls=%async_computation.19 | async-start | bytes 2621440 | tf_op jit(solution)/shard_map/reduce_scatter | solution.py:521
  522.2 161.2 %reduce-scatter.18.cloned.1.call-start = ((), (), s32[]{:S(2)}) async-start(), calls=%async_computation.15 | async-start | bytes 2621440 | tf_op jit(solution)/shard_map/reduce_scatter | solution.py:490
  527.3 205.3 %reduce-scatter.24.cloned.1.call-start = ((), (), s32[]{:S(2)}) async-start(), calls=%async_computation.20 | async-start | bytes 3538944 | tf_op jit(solution)/shard_map/reduce_scatter | solution.py:539
  554.6 83.3 %copy-start.9 = (f32[1,1024]{1,0:T(1,128)S(1)}, f32[1,1024]{1,0:T(1,128)}, u32[]{:S(2)}) copy-start(f32[1,1024]{1,0:T(1,128)} %copy-done.8) | copy-start | bytes 12292
  554.7 83.3 %copy-start.18 = (f32[256]{0:T(256)S(1)}, f32[256]{0:T(256)}, u32[]{:S(2)}) copy-start(f32[256]{0:T(256)} %copy-done.17) | copy-start | bytes 3076
  555.4 128.0 %copy-start.5 = (bf16[256,1024]{1,0:T(8,128)(2,1)S(1)}, bf16[256,1024]{1,0:T(8,128)(2,1)}, u32[]{:S(2)}) copy-start(bf16[256,1024]{1,0:T(8,128)(2,1)} %param.13) | copy-start | bytes 1572868
  555.4 128.0 %copy-start.6 = (bf16[256,1024]{1,0:T(8,128)(2,1)S(1)}, bf16[256,1024]{1,0:T(8,128)(2,1)}, u32[]{:S(2)}) copy-start(bf16[256,1024]{1,0:T(8,128)(2,1)} %reduce-scatter.20.cloned.1.call-done) | copy-start | bytes 1572868
  555.4 128.0 %copy-start.12 = (f32[256]{0:T(256)S(1)}, f32[256]{0:T(256)}, u32[]{:S(2)}) copy-start(f32[256]{0:T(256)} %copy-done.11) | copy-start | bytes 3076
  555.4 128.0 %copy-start.20 = (f32[256]{0:T(256)S(1)}, f32[256]{0:T(256)}, u32[]{:S(2)}) copy-start(f32[256]{0:T(256)} %copy-done.19) | copy-start | bytes 3076
  639.3 95.2 %copy-start.1 = (f32[2,8]{1,0:T(2,128)S(1)}, f32[2,8]{1,0:T(2,128)}, u32[]{:S(2)}) copy-start(f32[2,8]{1,0:T(2,128)} %param.19) | copy-start | bytes 196
  (25 other events, 336.8 us)
Sparse Core Ops, SparseCore 0:
  11.5 48.6 all-gather.9
  62.0 31.0 all-gather.11
  95.0 23.6 all-gather.13
  156.9 43.8 reduce-scatter.15
  202.7 30.9 all-gather.17
  235.8 45.9 all-gather.15
  283.8 24.0 all-gather.19
  309.5 45.9 all-gather.21
  368.4 42.5 reduce-scatter.19
  415.8 45.2 all-gather.23
  464.4 37.1 reduce-scatter.29
  504.9 44.8 reduce-scatter.27
  553.9 36.9 reduce-scatter.25
  593.1 44.7 reduce-scatter.21
  640.1 43.2 reduce-scatter.17
  687.0 45.5 reduce-scatter.23
